TPU v7x, 128 devices: a whole 4x4x4 slice. The times are simulated.
128 devices in a mesh: group: 16 (over y, z_hi, core), dom: 8 (over x, z_lo).
Axes of the slice: x: 4, y: 4, z: 4 (z_hi: 2, z_lo: 2; z = z_hi * 2 + z_lo), core: 2. Of those that a mesh axis runs over, the one named last changes fastest.
Arguments:
- head: float32 [16, 128, 128, 512], P('group', 'dom'), may hold values from -4 to 4
- conductivity: float32 [16, 128, 128, 512], P('group', 'dom'), may hold values from 0.2 to 2
- coarse_conductivity: float32 [16, 64, 64, 256], P('group', 'dom'), may hold values from 0.2 to 2
- pairing: int32 [16], replicated, may hold values from 0 to 15, as said below
Outputs:
- fine_next: float32 [16, 128, 128, 512], P('group', 'dom')
- coarse_next: float32 [16, 64, 64, 256], P('group', 'dom')
- difference: float32 [16, 64, 64, 256], P('group', 'dom')
Inputs may be any that keep to these rules, and one draw needn't show every extreme that they name: `pairing`: each sample index appears exactly once.
All inputs are finite; a program needn't handle non-finite values.
Results may differ from a plain program's by a relative error of at most 0.0003.
Values sent between devices are 32-bit elements; how exact they have to be, the bound alone decides.
A program may use at most 128 MiB of HBM per device.

v0:
```python
import jax
import jax.numpy as jnp
from jax import lax
from jax.sharding import PartitionSpec as P

alpha_vg = 1.5
theta_span = 0.4
storage = 0.5
step_dt = 0.05


def with_halo(shard, sides, width):
    for axis, dim in sides:
        devices, length = (lax.axis_size(axis), shard.shape[dim])
        up = [(i, (i + 1) % devices) for i in range(devices - 1)]
        down = [(j, i) for i, j in up]
        last = lax.slice_in_dim(shard, length - width, length, axis=dim)
        leading = lax.slice_in_dim(shard, 0, width, axis=dim)
        before = lax.ppermute(last, axis, up)
        after = lax.ppermute(leading, axis, down)
        shard = jnp.concatenate([before, shard, after], axis=dim)
    return shard


def closure(head, cond):
    neg = jnp.minimum(head, 0.0)
    usq = alpha_vg * neg * (alpha_vg * neg)
    wet = 1.0 / jnp.sqrt(1.0 + usq)
    rel = jnp.sqrt(wet) * (1.0 - jnp.sqrt(usq / (1.0 + usq))) ** 2
    cap = storage + theta_span * alpha_vg * alpha_vg * -neg * wet * wet * wet
    return (cond * rel, cap)


def advance(padded_h, padded_k, head, keff, cap, spacing):
    total = jnp.zeros_like(head)
    shifts = [
        ((2, None), (1, -1), (1, -1), 0.0),
        ((0, -2), (1, -1), (1, -1), 0.0),
        ((1, -1), (2, None), (1, -1), 0.0),
        ((1, -1), (0, -2), (1, -1), 0.0),
        ((1, -1), (1, -1), (2, None), spacing),
        ((1, -1), (1, -1), (0, -2), -spacing),
    ]
    for first, second, third, lift in shifts:
        near_h = padded_h[first[0] : first[1], second[0] : second[1], third[0] : third[1]]
        near_k = padded_k[first[0] : first[1], second[0] : second[1], third[0] : third[1]]
        total = total + 0.5 * (near_k + keff) * (near_h - head + lift)
    return head + step_dt * total / (spacing * spacing * cap)


def restrict(field):
    a, b, c = field.shape
    folded = field.reshape(a // 2, 2, b // 2, 2 * c)
    summed = folded[:, 0] + folded[:, 1]
    summed = summed[:, :, :c] + summed[:, :, c:]
    picker = (jnp.arange(c)[:, None] // 2 == jnp.arange(c // 2)[None, :]).astype(
        jnp.float32
    ) * 0.125
    return jnp.dot(
        summed, picker, precision=lax.Precision.HIGHEST, preferred_element_type=jnp.float32
    )


def side_pad(field):
    return jnp.pad(field, ((0, 0), (1, 1), (1, 1)))


def fine_step(head, cond):
    keff, cap = closure(head, cond)
    wide_h, wide_k = (with_halo(head, (("dom", 0),), 1), with_halo(keff, (("dom", 0),), 1))
    return advance(side_pad(wide_h), side_pad(wide_k), head, keff, cap, 1.0)


def coarse_step(head, cond):
    keff, cap = closure(head, cond)
    wide_h, wide_k = (with_halo(head, (("dom", 0),), 1), with_halo(keff, (("dom", 0),), 1))
    return advance(side_pad(wide_h), side_pad(wide_k), head, keff, cap, 2.0)


def deliver(blocks, pairing):
    mine = lax.axis_index("group")
    everyone = lax.all_gather(blocks[None], "group", axis=0, tiled=True)
    source = lax.dynamic_index_in_dim(pairing, mine, 0, keepdims=False)
    return lax.dynamic_index_in_dim(everyone, source, 0, keepdims=False)


def per_device(head, conductivity, coarse_conductivity, pairing):
    fine_head = head[0]
    start_small = restrict(fine_head)
    coarse_start = deliver(start_small[None], pairing)[0]
    fine_next = fine_step(fine_head, conductivity[0])
    coarse_next = coarse_step(coarse_start, coarse_conductivity[0])
    partner_next = deliver(restrict(fine_next)[None], pairing)[0]
    difference = partner_next - coarse_next
    return (fine_next[None], coarse_next[None], difference[None])


def solution(mesh):
    placed = (
        P("group", "dom", None, None),
        P("group", "dom", None, None),
        P("group", "dom", None, None),
        P(),
    )
    return jax.shard_map(
        per_device,
        mesh=mesh,
        in_specs=placed,
        out_specs=(
            P("group", "dom", None, None),
            P("group", "dom", None, None),
            P("group", "dom", None, None),
        ),
        check_vma=False,
    )
```

profile of v0, /device:TPU:1, one launch (start us, length us, event | category | flops | bytes accessed | tf_op | source)
XLA Modules:
  0.0 194.6 jit_solution(18150558024173943153)
XLA Ops:
  7.2 5.2 %reshape_squeeze.3 = f32[8,2,64,1024]{3,2,1,0:T(8,128)} reshape(f32[1,16,128,512]{3,2,1,0:T(8,128)} %param.4) | data formatting | bytes 8388608 | tf_op jit(solution)/shard_map/reshape;squeeze | solution.py:53
  12.4 2.6 %fusion.38 = f32[8,64,1024]{2,1,0:T(8,128)S(1)} fusion(f32[8,2,64,1024]{3,2,1,0:T(8,128)} %reshape_squeeze.3), kind=kLoop, calls=%fused_computation.65 | loop fusion | flops 524288 | bytes 6291456 | tf_op jit(solution)/shard_map/add | solution.py:54
  15.1 1.9 fusion.44
  17.1 7.0 %fusion.7 = f32[16,128,512]{2,1,0:T(8,128)S(1)} fusion(f32[1,16,128,512]{3,2,1,0:T(8,128)} %param.5, f32[1,16,128,512]{3,2,1,0:T(8,128)} %param.4), kind=kLoop, calls=%fused_computation.18 | loop fusion | flops 9437184 | bytes 12582912 | tf_op jit(solution)/shard_map/mul | solution.py:31
  24.1 1.3 collective-permute-start
  25.4 5.0 %collective-permute-start.2 = (f32[1,128,512]{2,1,0:T(8,128)S(1)}, f32[1,128,512]{2,1,0:T(8,128)S(1)}, u32[]{:S(2)}, u32[]{:S(2)}) collective-permute-start(f32[1,128,512]{2,1,0:T(8,128)S(1)} %get-tuple-element.9), channel_id=1, source_target_pairs={{0,1},{1,2},{2,3},{3,4},{4,5},{5,6},{6,7},{8,9},{9,10},{10,11},{11... | collective-permute-start | bytes 786440 | tf_op jit(solution)/shard_map/ppermute | solution.py:19
  30.5 1.3 collective-permute-start.1
  31.8 5.1 %collective-permute-start.3 = (f32[1,128,512]{2,1,0:T(8,128)S(1)}, f32[1,128,512]{2,1,0:T(8,128)S(1)}, u32[]{:S(2)}, u32[]{:S(2)}) collective-permute-start(f32[1,128,512]{2,1,0:T(8,128)S(1)} %get-tuple-element.11), channel_id=1, source_target_pairs={{0,1},{1,2},{2,3},{3,4},{4,5},{5,6},{6,7},{8,9},{9,10},{10,11},{11... | collective-permute-start | bytes 786440 | tf_op jit(solution)/shard_map/ppermute | solution.py:19
  36.9 15.3 %collective-permute-done.2 = f32[1,128,512]{2,1,0:T(8,128)S(1)} collective-permute-done((f32[1,128,512]{2,1,0:T(8,128)S(1)}, f32[1,128,512]{2,1,0:T(8,128)S(1)}, u32[]{:S(2)}, u32[]{:S(2)}) %collective-permute-start.2) | collective-permute-done | bytes 262176 | tf_op jit(solution)/shard_map/ppermute | solution.py:19
  52.2 4.7 %select_maximum_fusion.2 = f32[18,130,514]{2,1,0:T(8,128)S(1)} fusion(f32[1,128,512]{2,1,0:T(8,128)S(1)} %collective-permute-done, f32[16,128,512]{2,1,0:T(8,128)S(1)} %fusion.7, f32[1,128,512]{2,1,0:T(8,128)S(1)} %collective-permute-done.2), kind=kLoop, calls=%fused_computation.7 | loop fusion | flops 18041400 | bytes 9529632 | tf_op jit(solution)/shard_map/concatenate | solution.py:21
  57.9 4.7 %select_maximum_fusion = f32[18,130,514]{2,1,0:T(8,128)S(1)} fusion(f32[1,128,512]{2,1,0:T(8,128)S(1)} %collective-permute-done.1, f32[16,128,512]{2,1,0:T(8,128)S(1)} %bitcast.61, f32[1,128,512]{2,1,0:T(8,128)S(1)} %collective-permute-done.3), kind=kLoop, calls=%fused_computation.5 | loop fusion | flops 18041400 | bytes 9529632 | tf_op jit(solution)/shard_map/concatenate | solution.py:21
  62.6 15.3 %fusion.10 = f32[16,128,512]{2,1,0:T(8,128)} fusion(f32[16,128,512]{2,1,0:T(8,128)S(1)} %bitcast.62, f32[18,130,514]{2,1,0:T(8,128)S(1)} %select_maximum_fusion, f32[16,128,512]{2,1,0:T(8,128)} %copy-done.1, f32[18,130,514]{2,1,0:T(8,128)S(1)} %select_maximum_fusion.2, f32[1,128,512]{2,1,0:T(8,128)S(1)} %collective-permute-done.3, ...), kind=kLoop, calls=%fused_computation.21 | loop fusion | flops 50331648 | bytes 47185920 | tf_op jit(solution)/shard_map/add | solution.py:48
  77.9 5.3 %reshape.54 = f32[8,2,64,1024]{3,2,1,0:T(8,128)} reshape(f32[16,128,512]{2,1,0:T(8,128)} %fusion.10) | data formatting | bytes 8388608 | tf_op jit(solution)/shard_map/reshape | solution.py:53
  83.2 2.7 %fusion.36 = f32[8,64,1024]{2,1,0:T(8,128)S(1)} fusion(f32[8,2,64,1024]{3,2,1,0:T(8,128)} %reshape.54), kind=kLoop, calls=%fused_computation.61 | loop fusion | flops 524288 | bytes 6291456 | tf_op jit(solution)/shard_map/add | solution.py:54
  85.9 1.9 fusion.42
  90.4 19.3 %all-gather.5.cloned.1.call-done = f32[128,64,256]{2,1,0:T(8,128)} async-done(((f32[8,64,256]{2,1,0:T(8,128)}), f32[128,64,256]{2,1,0:T(8,128)}) %all-gather.5.cloned.1.call-update) | async-done | bytes 8388624 | tf_op jit(solution)/shard_map/all_gather | solution.py:82
  109.7 1.5 fusion.50
  111.2 1.3 collective-permute-start.4
  112.5 4.0 %collective-permute-start.6 = (f32[1,64,256]{2,1,0:T(8,128)S(1)}, f32[1,64,256]{2,1,0:T(8,128)S(1)}, u32[]{:S(2)}, u32[]{:S(2)}) collective-permute-start(f32[1,64,256]{2,1,0:T(8,128)S(1)} %get-tuple-element.13), channel_id=1, source_target_pairs={{0,1},{1,2},{2,3},{3,4},{4,5},{5,6},{6,7},{8,9},{9,10},{10,11},{11... | collective-permute-start | bytes 196616 | tf_op jit(solution)/shard_map/ppermute | solution.py:19
  117.4 1.3 collective-permute-start.5
  118.7 4.0 %collective-permute-start.7 = (f32[1,64,256]{2,1,0:T(8,128)S(1)}, f32[1,64,256]{2,1,0:T(8,128)S(1)}, u32[]{:S(2)}, u32[]{:S(2)}) collective-permute-start(f32[1,64,256]{2,1,0:T(8,128)S(1)} %get-tuple-element.7), channel_id=1, source_target_pairs={{0,1},{1,2},{2,3},{3,4},{4,5},{5,6},{6,7},{8,9},{9,10},{10,11},{11... | collective-permute-start | bytes 196616 | tf_op jit(solution)/shard_map/ppermute | solution.py:19
  123.1 3.3 %collective-permute-done.7 = f32[1,64,256]{2,1,0:T(8,128)S(1)} collective-permute-done((f32[1,64,256]{2,1,0:T(8,128)S(1)}, f32[1,64,256]{2,1,0:T(8,128)S(1)}, u32[]{:S(2)}, u32[]{:S(2)}) %collective-permute-start.7) | collective-permute-done | bytes 65568 | tf_op jit(solution)/shard_map/ppermute | solution.py:19
  126.7 57.8 %all-gather.7.cloned.1.call-done = f32[128,64,256]{2,1,0:T(8,128)} async-done(((f32[8,64,256]{2,1,0:T(8,128)}), f32[128,64,256]{2,1,0:T(8,128)}) %all-gather.7.cloned.1.call-update) | async-done | bytes 8388624 | tf_op jit(solution)/shard_map/all_gather | solution.py:82
  184.5 3.3 %fusion.79 = (f32[1,8,64,256]{3,2,1,0:T(8,128)}, f32[8,64,256]{2,1,0:T(8,128)}) fusion(f32[16,1,8,64,256]{4,3,2,0,1:T(8,128)} %bitcast.67, s32[]{:T(128)S(6)} %select_n.25, f32[8,64,256]{2,1,0:T(8,128)S(1)} %get-tuple-element.6, f32[10,66,258]{2,1,0:T(8,128)S(1)} %select_maximum_fusion.4, f32[8,64,256]{2,1,0:T(8,128)S(1)} %get-tuple-element.5, ...), kind=kLoop, calls=%fused_computation.133 | loop fusion | flops 6553600 | bytes 7077892 | tf_op jit(solution)/shard_map/broadcast_in_dim | solution.py:95
  (26 shorter events, 3.5 us)
Async XLA Ops:
  7.2 102.5 %all-gather.5.cloned.1.call-start = ((), (), s32[]{:S(2)}) async-start(), calls=%async_computation | async-start | bytes 8912896 | tf_op jit(solution)/shard_map/all_gather | solution.py:82
  17.0 167.5 %all-gather.7.cloned.1.call-start = ((), (), s32[]{:S(2)}) async-start(), calls=%async_computation.1 | async-start | bytes 8912896 | tf_op jit(solution)/shard_map/all_gather | solution.py:82
  17.0 13.4 %copy-start = (f32[1,16,128,512]{3,2,1,0:T(8,128)S(1)}, f32[1,16,128,512]{3,2,1,0:T(8,128)}, u32[]{:S(2)}) copy-start(f32[1,16,128,512]{3,2,1,0:T(8,128)} %param.4) | copy-start | bytes 12582916
  24.0 32.8 %copy-start.1 = (f32[16,128,512]{2,1,0:T(8,128)}, f32[16,128,512]{2,1,0:T(8,128)S(1)}, u32[]{:S(2)}) copy-start(f32[16,128,512]{2,1,0:T(8,128)S(1)} %fusion.7) | copy-start | bytes 12582916
  24.1 12.8 %collective-permute-start = (f32[1,128,512]{2,1,0:T(8,128)S(1)}, f32[1,128,512]{2,1,0:T(8,128)S(1)}, u32[]{:S(2)}, u32[]{:S(2)}) collective-permute-start(f32[1,128,512]{2,1,0:T(8,128)S(1)} %get-tuple-element.10), channel_id=1, source_target_pairs={{1,0},{2,1},{3,2},{4,3},{5,4},{6,5},{7,6},{9,8},{10,9},{11,10},{12... | collective-permute-start | bytes 786440 | tf_op jit(solution)/shard_map/ppermute | solution.py:20
  25.4 26.8 %collective-permute-start.2 = (f32[1,128,512]{2,1,0:T(8,128)S(1)}, f32[1,128,512]{2,1,0:T(8,128)S(1)}, u32[]{:S(2)}, u32[]{:S(2)}) collective-permute-start(f32[1,128,512]{2,1,0:T(8,128)S(1)} %get-tuple-element.9), channel_id=1, source_target_pairs={{0,1},{1,2},{2,3},{3,4},{4,5},{5,6},{6,7},{8,9},{9,10},{10,11},{11... | collective-permute-start | bytes 786440 | tf_op jit(solution)/shard_map/ppermute | solution.py:19
  30.5 26.4 %collective-permute-start.1 = (f32[1,128,512]{2,1,0:T(8,128)S(1)}, f32[1,128,512]{2,1,0:T(8,128)S(1)}, u32[]{:S(2)}, u32[]{:S(2)}) collective-permute-start(f32[1,128,512]{2,1,0:T(8,128)S(1)} %get-tuple-element.12), channel_id=1, source_target_pairs={{1,0},{2,1},{3,2},{4,3},{5,4},{6,5},{7,6},{9,8},{10,9},{11,10},{12... | collective-permute-start | bytes 786440 | tf_op jit(solution)/shard_map/ppermute | solution.py:20
  31.8 26.1 %collective-permute-start.3 = (f32[1,128,512]{2,1,0:T(8,128)S(1)}, f32[1,128,512]{2,1,0:T(8,128)S(1)}, u32[]{:S(2)}, u32[]{:S(2)}) collective-permute-start(f32[1,128,512]{2,1,0:T(8,128)S(1)} %get-tuple-element.11), channel_id=1, source_target_pairs={{0,1},{1,2},{2,3},{3,4},{4,5},{5,6},{6,7},{8,9},{9,10},{10,11},{11... | collective-permute-start | bytes 786440 | tf_op jit(solution)/shard_map/ppermute | solution.py:19
  83.2 4.6 %copy-start.3 = (s32[16]{0:T(128)S(1)}, s32[16]{0:T(128)}, u32[]{:S(2)}) copy-start(s32[16]{0:T(128)} %param.7) | copy-start | bytes 196
  83.2 26.5 %copy-start.2 = (f32[1,8,64,256]{3,2,1,0:T(8,128)S(1)}, f32[1,8,64,256]{3,2,1,0:T(8,128)}, u32[]{:S(2)}) copy-start(f32[1,8,64,256]{3,2,1,0:T(8,128)} %param.6) | copy-start | bytes 1572868
  111.2 11.5 %collective-permute-start.4 = (f32[1,64,256]{2,1,0:T(8,128)S(1)}, f32[1,64,256]{2,1,0:T(8,128)S(1)}, u32[]{:S(2)}, u32[]{:S(2)}) collective-permute-start(f32[1,64,256]{2,1,0:T(8,128)S(1)} %get-tuple-element.14), channel_id=1, source_target_pairs={{1,0},{2,1},{3,2},{4,3},{5,4},{6,5},{7,6},{9,8},{10,9},{11,10},{12... | collective-permute-start | bytes 196616 | tf_op jit(solution)/shard_map/ppermute | solution.py:20
  112.5 10.2 %collective-permute-start.6 = (f32[1,64,256]{2,1,0:T(8,128)S(1)}, f32[1,64,256]{2,1,0:T(8,128)S(1)}, u32[]{:S(2)}, u32[]{:S(2)}) collective-permute-start(f32[1,64,256]{2,1,0:T(8,128)S(1)} %get-tuple-element.13), channel_id=1, source_target_pairs={{0,1},{1,2},{2,3},{3,4},{4,5},{5,6},{6,7},{8,9},{9,10},{10,11},{11... | collective-permute-start | bytes 196616 | tf_op jit(solution)/shard_map/ppermute | solution.py:19
  117.4 5.7 %collective-permute-start.5 = (f32[1,64,256]{2,1,0:T(8,128)S(1)}, f32[1,64,256]{2,1,0:T(8,128)S(1)}, u32[]{:S(2)}, u32[]{:S(2)}) collective-permute-start(f32[1,64,256]{2,1,0:T(8,128)S(1)} %get-tuple-element.8), channel_id=1, source_target_pairs={{1,0},{2,1},{3,2},{4,3},{5,4},{6,5},{7,6},{9,8},{10,9},{11,10},{12... | collective-permute-start | bytes 196616 | tf_op jit(solution)/shard_map/ppermute | solution.py:20
  118.7 7.7 %collective-permute-start.7 = (f32[1,64,256]{2,1,0:T(8,128)S(1)}, f32[1,64,256]{2,1,0:T(8,128)S(1)}, u32[]{:S(2)}, u32[]{:S(2)}) collective-permute-start(f32[1,64,256]{2,1,0:T(8,128)S(1)} %get-tuple-element.7), channel_id=1, source_target_pairs={{0,1},{1,2},{2,3},{3,4},{4,5},{5,6},{6,7},{8,9},{9,10},{10,11},{11... | collective-permute-start | bytes 196616 | tf_op jit(solution)/shard_map/ppermute | solution.py:19
Sparse Core Ops, SparseCore 0:
  17.1 92.5 all-gather.4
  112.6 71.8 all-gather.6
where the time goes:
time: 195 us
  waiting for transfers between devices  96.8 us (50%)
  other arithmetic  42.4 us (22%)
  starting transfers between devices  23.3 us (12%)
  between operations  16.2 us (8%)
  local copies, waits for them, and re-layouts  12.1 us (6%)
  matrix products  3.82 us (2%)
    all_gather x2, waiting for transfers between devices, deliver(): everyone = lax.all_gather(blocks[None], 'group', axis=0, tiled=True)  77.1 us
    ppermute x4, waiting for transfers between devices, with_halo(): before = lax.ppermute(last, axis, up)  19.6 us
    ppermute x4, starting transfers between devices, with_halo(): before = lax.ppermute(last, axis, up)  18.1 us
    add x1, other arithmetic, advance(): return head + step_dt * total / (spacing * spacing * cap)  15.3 us
    concatenate x4, other arithmetic, with_halo(): shard = jnp.concatenate([before, shard, after], axis=dim)  10.1 us
    mul x2, other arithmetic, closure(): return (cond * rel, cap)  8.46 us
    reshape x1, local copies, waits for them, and re-layouts, restrict(): folded = field.reshape(a // 2, 2, b // 2, 2 * c)  5.29 us
    add x2, other arithmetic, restrict(): summed = folded[:, 0] + folded[:, 1]  5.29 us
  transfers between devices with their start and end apart: 10, of which 5 were waited for; matrix products, arithmetic and copies ran while one was open for 23% of the time, Pallas kernels for 0%

commit v1 on v0

v1 whole, which is shorter than its diff:
```python
import functools

import jax
import jax.numpy as jnp
from jax import lax
from jax.experimental import pallas as pl
from jax.experimental.pallas import tpu as pltpu
from jax.sharding import PartitionSpec as P

MESH = pl.DeviceIdType.MESH
F32 = jnp.float32
NP = 8
CAP = 8

TOP = 8
CH = 32


def place(layer):
    return {0: 0, 7: 1}.get(layer, layer + 1)


def closure(h, cond, spacing):
    t = 1.5 * jnp.minimum(h, 0.0)
    r = lax.rsqrt(1.0 + t * t)
    p = t * r
    a = 1.0 + p
    k = cond * (r * lax.rsqrt(r) * (a * a))
    s2 = spacing * spacing
    w = 1.0 / (20.0 * s2 - (24.0 * s2) * (p * (r * r)))
    return k, w


def in_layer(hb, kb, x, row, rows, spacing):
    ha = hb[x, pl.ds(row, rows + 16), :]
    ka = kb[x, pl.ds(row, rows + 16), :]
    h, k = ha[8 : 8 + rows], ka[8 : 8 + rows]
    tot = (ka[9 : 9 + rows] + k) * (ha[9 : 9 + rows] - h)
    hd, kd = ha[7 : 7 + rows], ka[7 : 7 + rows]
    tot = tot + (kd + k) * (hd - h)
    n = h.shape[1]
    lane = lax.broadcasted_iota(jnp.int32, h.shape, 1)
    hz = jnp.where(lane == n - 1, 0.0, pltpu.roll(h, n - 1, 1))
    kz = jnp.where(lane == n - 1, 0.0, pltpu.roll(k, n - 1, 1))
    hs = h - spacing
    fz = (kz + k) * (hz - hs)
    fd = jnp.where(lane == 0, k * (h + spacing), pltpu.roll(fz, 1, 1))
    return h, k, tot + (fz - fd)


def kernel(cap, pairing, head, cond, ccond, fine_out, coarse_out, diff_out,
           hb, kb, wb, fx, f01, frecv, vs, pick,
           sbuf, sab, sx, sy, sc, sd, nbuf, nab, nx, ny, nc, nd, bbuf, bab, bx, by, bc, bd,
           ch, ck, cw, cfx, cf01, cfrecv, dbuf,
           hsem, ksem, csem, osem, halo_s, halo_r, sa_s, sa_r, na_s, na_r, ba_s, ba_r, sc_s, sc_r, nc_s, nc_r, bc_s, bc_r,
           cross_s, cross_r):
    g = lax.axis_index("group")
    d = lax.axis_index("dom")
    zh = lax.rem(g // 2, 2)
    me = (g // 4) * 2 + lax.rem(g, 2)

    def index_of(j, plane):
        return (j // 2) * 4 + plane * 2 + lax.rem(j, 2)

    def mate(s):
        j = lax.rem(me + s, NP)
        return j, index_of(j, zh)

    other = index_of(me, 1 - zh)
    last = 7

    def load(src, dst, sem):
        return pltpu.make_async_copy(src, dst, sem)

    def hload(l):
        return load(head.at[0, pl.ds(2 * l, 2)], hb.at[pl.ds(2 * l, 2), pl.ds(TOP, 128), :], hsem.at[l])

    def kload(l):
        return load(cond.at[0, pl.ds(2 * l, 2)], kb.at[pl.ds(2 * l, 2), pl.ds(TOP, 128), :], ksem.at[l])

    cload = load(ccond.at[0], ck.at[pl.ds(0, 8), pl.ds(8, 64), :], csem)
    hload(0).start()
    kload(0).start()
    for l in range(1, 8):
        hload(l).start()
    for l in range(1, 8):
        kload(l).start()
    cload.start()

    bar = pltpu.get_barrier_semaphore()

    def greet(g2, d2):
        pl.semaphore_signal(bar, inc=1, device_id=(g2, d2), device_id_type=MESH)

    for s in range(1, NP):
        greet(mate(s)[1], d)
    greet(other, d)

    @pl.when(d > 0)
    def _():
        greet(g, d - 1)

    @pl.when(d < last)
    def _():
        greet(g, d + 1)

    z8 = jnp.zeros((8, 512), F32)
    zc = jnp.zeros((8, 256), F32)

    def pads(x, _):
        for b in (hb, kb):
            b[x, 0:8, :] = z8
            b[x, 136:144, :] = z8
        return 0

    lax.fori_loop(0, 16, pads, 0)

    def cpads(x, _):
        for b in (ch, ck):
            b[x, 0:8, :] = zc
            b[x, 72:80, :] = zc
        return 0

    lax.fori_loop(0, 8, cpads, 0)
    pi = lax.broadcasted_iota(jnp.int32, (256, 128), 0)
    pj = lax.broadcasted_iota(jnp.int32, (256, 128), 1)
    pick[...] = jnp.where(pi // 2 == pj, 0.125, 0.0).astype(jnp.bfloat16)

    @pl.when(d == last)
    def _():
        def zero(i, _):
            hb[16, pl.ds(TOP + i * 8, 8), :] = z8
            kb[16, pl.ds(TOP + i * 8, 8), :] = z8
            return 0

        lax.fori_loop(0, 16, zero, 0)

        def czero(i, _):
            ch[8, pl.ds(8 + i * 8, 8), :] = zc
            ck[8, pl.ds(8 + i * 8, 8), :] = zc
            return 0

        lax.fori_loop(0, 8, czero, 0)

    cross = [jnp.int32(0)] * cap
    count = jnp.int32(0)
    for j in range(NP):
        p = pairing[index_of(j, 1 - zh)]
        mine = lax.rem(p // 2, 2) == zh
        slot = (p // 4) * 2 + lax.rem(p, 2)
        for i in range(cap):
            cross[i] = jnp.where(mine & (count == i), slot, cross[i])
        count = count + jnp.where(mine, 1, 0)
    where = []
    count = jnp.int32(0)
    for j in range(NP):
        p = pairing[index_of(j, zh)]
        mine = lax.rem(p // 2, 2) == zh
        where.append((mine, (p // 4) * 2 + lax.rem(p, 2), jnp.minimum(count, cap - 1)))
        count = count + jnp.where(mine, 0, 1)

    def close_layer(x):
        def body(i, _):
            r = pl.multiple_of(i * CH, CH)
            k, w = closure(hb[x, pl.ds(TOP + r, CH), :], kb[x, pl.ds(TOP + r, CH), :], 1.0)
            kb[x, pl.ds(TOP + r, CH), :] = k
            wb[x, pl.ds(r, CH), :] = w
            return 0

        lax.fori_loop(0, 128 // CH, body, 0)

    hload(0).wait()
    kload(0).wait()
    close_layer(0)
    pl.semaphore_wait(bar, NP + jnp.where(d > 0, 1, 0) + jnp.where(d < last, 1, 0))

    def remote(src, dst, ssem, rsem, g2, d2):
        return pltpu.make_async_remote_copy(src_ref=src, dst_ref=dst, send_sem=ssem, recv_sem=rsem,
                                            device_id=(g2, d2), device_id_type=MESH)

    down = d - 1
    upper = d + 1
    rows = pl.ds(TOP, 128)
    halo_h = remote(hb.at[0, rows, :], hb.at[16, rows, :], halo_s.at[0], halo_r.at[0], g, down)
    halo_k = remote(kb.at[0, rows, :], kb.at[16, rows, :], halo_s.at[1], halo_r.at[1], g, down)
    halo_f = remote(fx, frecv, halo_s.at[2], halo_r.at[2], g, upper)
    crow = pl.ds(8, 64)
    chalo_h = remote(ch.at[0, crow, :], ch.at[8, crow, :], halo_s.at[3], halo_r.at[3], g, down)
    chalo_k = remote(ck.at[0, crow, :], ck.at[8, crow, :], halo_s.at[4], halo_r.at[4], g, down)
    chalo_f = remote(cfx, cfrecv, halo_s.at[5], halo_r.at[5], g, upper)

    @pl.when(d > 0)
    def _():
        halo_h.start()
        halo_k.start()

    def restrict(a, b, store):
        for r in range(0, 128, CH):
            s = a(r) + b(r)
            for q in range(4):
                vs[q, r : r + CH, :] = s[:, q * 128 : (q + 1) * 128]
        for half in range(2):
            parts = [vs[q, pl.ds(0, 64, 2), :] + vs[q, pl.ds(1, 64, 2), :] for q in (2 * half, 2 * half + 1)]
            e = jnp.concatenate(parts, axis=1)
            hi = e.astype(jnp.bfloat16)
            lo = (e - hi.astype(F32)).astype(jnp.bfloat16)
            w = pick[...]
            o = jnp.dot(hi, w, preferred_element_type=F32) + jnp.dot(lo, w, preferred_element_type=F32)
            store(half, o)

    def into(buf, pos):
        def store(half, o):
            buf[:, pos, :, half * 128 : (half + 1) * 128] = o.reshape(8, 8, 128)

        return store

    def a_copy(s, buf, ab, ssem, rsem):
        j, g2 = mate(s)
        return remote(buf.at[j], ab.at[me], ssem.at[s - 1], rsem.at[s - 1], g2, d)

    def a_start(buf, ab, ssem, rsem):
        for s in range(1, NP):
            a_copy(s, buf, ab, ssem, rsem).start()
        ab[me] = buf[me]

    def a_wait(buf, ab, ssem, rsem):
        for s in range(1, NP):
            a_copy(s, buf, ab, ssem, rsem).wait()

    def b_copy(i, x, y):
        return remote(x, y, cross_s.at[i], cross_r.at[i], other, d)

    def b_start(i, x, y, ab):
        for n in range(cap):
            x[n] = ab[cross[n]]
        b_copy(i, x, y).start()

    def c_copy(s, buf, to, ssem, rsem):
        j, g2 = mate(s)
        return remote(buf.at[j], to.at[me], ssem.at[s - 1], rsem.at[s - 1], g2, d)

    def c_start(ab, y, buf, to, ssem, rsem):
        for j in range(NP):
            mine, slot, crossed = where[j]
            buf[j] = jnp.where(mine, ab[slot], y[crossed])
        for s in range(1, NP):
            c_copy(s, buf, to, ssem, rsem).start()
        to[me] = buf[me]

    def c_wait(buf, to, ssem, rsem):
        for s in range(1, NP):
            c_copy(s, buf, to, ssem, rsem).wait()

    for l in range(8):
        if l:
            hload(l).wait()
        restrict(lambda r: hb[2 * l, pl.ds(TOP + r, CH), :], lambda r: hb[2 * l + 1, pl.ds(TOP + r, CH), :], into(sbuf, place(l)))
    a_start(sbuf, sab, sa_s, sa_r)

    def face(x, r):
        here, there = (x, pl.ds(TOP + r, CH), slice(None)), (x + 1, pl.ds(TOP + r, CH), slice(None))
        return (kb[there] + kb[here]) * (hb[there] - hb[here])

    def step_layer(x):
        def body(i, _):
            r = pl.multiple_of(i * CH, CH)
            h, k, tot = in_layer(hb, kb, x, r, CH, 1.0)
            f = (kb[x + 1, pl.ds(TOP + r, CH), :] + k) * (hb[x + 1, pl.ds(TOP + r, CH), :] - h)
            tot = tot + (f - fx[pl.ds(r, CH), :])
            fx[pl.ds(r, CH), :] = f
            wb[x, pl.ds(r, CH), :] = h + tot * wb[x, pl.ds(r, CH), :]
            return 0

        lax.fori_loop(0, 128 // CH, body, 0)

    def out_pair(l):
        return load(wb.at[pl.ds(2 * l, 2)], fine_out.at[0, pl.ds(2 * l, 2)], osem.at[l])

    def out_row(x):
        return lambda r: wb[x, pl.ds(r, CH), :]

    def next_small(l, buf, pos):
        restrict(out_row(2 * l), out_row(2 * l + 1), into(buf, pos))
        out_pair(l).start()

    close_layer(1)

    def first_face(i, _):
        r = pl.multiple_of(i * CH, CH)
        f = face(0, r)
        f01[pl.ds(r, CH), :] = f
        fx[pl.ds(r, CH), :] = f
        return 0

    lax.fori_loop(0, 128 // CH, first_face, 0)
    kload(1).wait()
    close_layer(2)
    step_layer(1)
    for l in range(1, 7):
        close_layer(2 * l + 1)
        step_layer(2 * l)
        kload(l + 1).wait()
        close_layer(2 * l + 2)
        step_layer(2 * l + 1)
        next_small(l, nbuf, l - 1)
        if l == 3:
            a_wait(sbuf, sab, sa_s, sa_r)
            b_start(0, sx, sy, sab)
    a_start(nbuf, nab, na_s, na_r)
    b_copy(0, sx, sy).wait()
    c_start(sab, sy, sc, sd, sc_s, sc_r)
    close_layer(15)
    step_layer(14)

    @pl.when(d < last)
    def _():
        halo_h.wait_recv()
        halo_k.wait_recv()

    step_layer(15)

    @pl.when(d < last)
    def _():
        halo_f.start()

    next_small(7, bbuf, 1)
    a_wait(nbuf, nab, na_s, na_r)
    b_start(1, nx, ny, nab)

    c_wait(sc, sd, sc_s, sc_r)
    cload.wait()

    def close_coarse(l):
        h = sd[:, place(l)].reshape(64, 256)
        k, w = closure(h, ck[l, crow, :], 2.0)
        ch[l, crow, :] = h
        ck[l, crow, :] = k
        cw[l] = w

    close_coarse(0)

    @pl.when(d > 0)
    def _():
        chalo_h.start()
        chalo_k.start()

    for l in range(1, 8):
        close_coarse(l)

    @pl.when(d > 0)
    def _():
        halo_f.wait_recv()

    @pl.when(d == 0)
    def _():
        def edge(i, _):
            r = pl.multiple_of(i * CH, CH)
            frecv[pl.ds(r, CH), :] = hb[0, pl.ds(TOP + r, CH), :] * kb[0, pl.ds(TOP + r, CH), :]
            return 0

        lax.fori_loop(0, 128 // CH, edge, 0)

    def lowest(i, _):
        r = pl.multiple_of(i * CH, CH)
        h, k, tot = in_layer(hb, kb, 0, r, CH, 1.0)
        tot = tot + (f01[pl.ds(r, CH), :] - frecv[pl.ds(r, CH), :])
        wb[0, pl.ds(r, CH), :] = h + tot * wb[0, pl.ds(r, CH), :]
        return 0

    lax.fori_loop(0, 128 // CH, lowest, 0)
    next_small(0, bbuf, 0)
    a_start(bbuf, bab, ba_s, ba_r)

    b_copy(1, nx, ny).wait()
    c_start(nab, ny, nc, nd, nc_s, nc_r)

    def cface(x):
        return (ck[x + 1, crow, :] + ck[x, crow, :]) * (ch[x + 1, crow, :] - ch[x, crow, :])

    def step_coarse(x):
        h, k, tot = in_layer(ch, ck, x, 0, 64, 2.0)
        f = cface(x)
        tot = tot + (f - cfx[...])
        cfx[...] = f
        cw[x] = h + tot * cw[x]

    f = cface(0)
    cf01[...] = f
    cfx[...] = f
    for x in range(1, 7):
        step_coarse(x)

    @pl.when(d < last)
    def _():
        chalo_h.wait_recv()
        chalo_k.wait_recv()

    step_coarse(7)

    @pl.when(d < last)
    def _():
        chalo_f.start()

    a_wait(bbuf, bab, ba_s, ba_r)
    b_start(2, bx, by, bab)

    @pl.when(d > 0)
    def _():
        chalo_f.wait_recv()

    @pl.when(d == 0)
    def _():
        cfrecv[...] = ch[0, crow, :] * ck[0, crow, :]

    h, k, tot = in_layer(ch, ck, 0, 0, 64, 2.0)
    tot = tot + (cf01[...] - cfrecv[...])
    cw[0] = h + tot * cw[0]
    cout = load(cw, coarse_out.at[0], csem)
    cout.start()
    b_copy(2, bx, by).wait()
    c_start(bab, by, bc, bd, bc_s, bc_r)
    c_wait(nc, nd, nc_s, nc_r)
    for l in range(1, 7):
        dbuf[l] = nd[:, l - 1].reshape(64, 256) - cw[l]
    c_wait(bc, bd, bc_s, bc_r)
    dbuf[0] = bd[:, 0].reshape(64, 256) - cw[0]
    dbuf[7] = bd[:, 1].reshape(64, 256) - cw[7]
    dout = load(dbuf, diff_out.at[0], ksem.at[0])
    dout.start()

    @pl.when(d > 0)
    def _():
        halo_h.wait_send()
        halo_k.wait_send()
        chalo_h.wait_send()
        chalo_k.wait_send()

    @pl.when(d < last)
    def _():
        halo_f.wait_send()
        chalo_f.wait_send()

    for l in range(8):
        out_pair(l).wait()
    cout.wait()
    dout.wait()


def payload(cap, layers):
    piece = (layers, 8, 256)
    return [
        pltpu.VMEM((NP,) + piece, F32),
        pltpu.VMEM((NP,) + piece, F32),
        pltpu.VMEM((cap,) + piece, F32),
        pltpu.VMEM((cap,) + piece, F32),
        pltpu.VMEM((NP,) + piece, F32),
        pltpu.VMEM((NP,) + piece, F32),
    ]


def run(cap, pairing, head, cond, ccond):
    dma = pltpu.SemaphoreType.DMA
    scratch = [
        pltpu.VMEM((17, 144, 512), F32),
        pltpu.VMEM((17, 144, 512), F32),
        pltpu.VMEM((16, 128, 512), F32),
        pltpu.VMEM((128, 512), F32),
        pltpu.VMEM((128, 512), F32),
        pltpu.VMEM((128, 512), F32),
        pltpu.VMEM((4, 128, 128), F32),
        pltpu.VMEM((256, 128), jnp.bfloat16),
        *payload(cap, 8),
        *payload(cap, 6),
        *payload(cap, 2),
        pltpu.VMEM((9, 80, 256), F32),
        pltpu.VMEM((9, 80, 256), F32),
        pltpu.VMEM((8, 64, 256), F32),
        pltpu.VMEM((64, 256), F32),
        pltpu.VMEM((64, 256), F32),
        pltpu.VMEM((64, 256), F32),
        pltpu.VMEM((8, 64, 256), F32),
        dma((8,)), dma((8,)), dma, dma((8,)), dma((6,)), dma((6,)),
        *[dma((NP - 1,))] * 12,
        dma((3,)), dma((3,)),
    ]
    anywhere = pl.BlockSpec(memory_space=pl.ANY)
    return pl.pallas_call(
        functools.partial(kernel, cap),
        out_shape=(
            jax.ShapeDtypeStruct(head.shape, F32),
            jax.ShapeDtypeStruct(ccond.shape, F32),
            jax.ShapeDtypeStruct(ccond.shape, F32),
        ),
        in_specs=[pl.BlockSpec(memory_space=pltpu.SMEM), anywhere, anywhere, anywhere],
        out_specs=(anywhere, anywhere, anywhere),
        scratch_shapes=scratch,
        compiler_params=pltpu.CompilerParams(
            collective_id=0, has_side_effects=True, vmem_limit_bytes=48 * 2**20
        ),
    )(pairing, head, cond, ccond)


def per_device(head, conductivity, coarse_conductivity, pairing):
    return run(CAP, pairing, head, conductivity, coarse_conductivity)


def solution(mesh):
    block = P("group", "dom", None, None)
    return jax.shard_map(
        per_device,
        mesh=mesh,
        in_specs=(block, block, block, P()),
        out_specs=(block, block, block),
        check_vma=False,
    )
```

time: 195 us -> 72.8 us (0.37)
  waiting for transfers between devices: 96.8 us -> 0 us
  Pallas kernels: 0 us -> 66.7 us
  other arithmetic: 42.4 us -> 0 us
  starting transfers between devices: 23.3 us -> 0 us
  between operations: 16.2 us -> 0.65 us
  local copies, waits for them, and re-layouts: 12.1 us -> 5.29 us
  matrix products: 3.82 us -> 0 us
    all_gather x2 -> x0, waiting for transfers between devices: 77.1 us -> none  [deliver(): everyone = lax.all_gather(blocks[None], 'group', axis=0, tiled=True)]
    pallas_call x0 -> x1, Pallas kernels: none -> 66.7 us  [run(): pl.pallas_call(functools.partial(kernel, cap), out_shape=(jax.ShapeDtypeS...]
    ppermute x8 -> x0, starting transfers between devices: 23.2 us -> none  [the longest x4 18.1 us: with_halo(): before = lax.ppermute(last, axis, up)]
    add x3 -> x0, other arithmetic: 20.6 us -> none  [the longest x1 15.3 us: advance(): return head + step_dt * total / (spacing * spacing * cap)]
    ppermute x8 -> x0, waiting for transfers between devices: 19.6 us -> none  [the longest x4 19.6 us: with_halo(): before = lax.ppermute(last, axis, up)]
    concatenate x4 -> x0, other arithmetic: 10.1 us -> none  [with_halo(): shard = jnp.concatenate([before, shard, after], axis=dim)]
    mul x2 -> x0, other arithmetic: 8.46 us -> none  [closure(): return (cond * rel, cap)]
    reshape x1 -> x0, local copies, waits for them, and re-layouts: 5.29 us -> none  [restrict(): folded = field.reshape(a // 2, 2, b // 2, 2 * c)]
  transfers between devices with their start and end apart: 10 -> 0, of which waited for: 5 -> 0; matrix products, arithmetic and copies ran while one was open for 23% -> 0% of each run, Pallas kernels for 0% -> 0%
where the time goes in v1:
time: 72.8 us; the launch traced here: 72.7 us
  Pallas kernels  66.7 us (92%)
  local copies, waits for them, and re-layouts  5.29 us (7%)
    pallas_call x1, Pallas kernels, run(): pl.pallas_call(functools.partial(kernel, cap), out_shape=(jax.ShapeDtypeS...  66.7 us
    unnamed x7, local copies, waits for them, and re-layouts  5.29 us

profile of v1, /device:TPU:1, one launch (start us, length us, event | category | flops | bytes accessed | tf_op | source)
XLA Modules:
  0.0 72.7 jit_solution(954481495064223064)
XLA Ops:
  0.6 0.0 copy-start
  0.6 1.0 %copy-done = f32[1,8,64,256]{3,2,1,0:T(8,128)S(1)} copy-done((f32[1,8,64,256]{3,2,1,0:T(8,128)S(1)}, f32[1,8,64,256]{3,2,1,0:T(8,128)}, u32[]{:S(2)}) %copy-start) | copy-done | bytes 524312
  1.7 0.0 copy-start.1
  1.7 0.7 copy-done.1
  2.3 66.7 %shard_map.67 = (f32[1,16,128,512]{3,2,1,0:T(8,128)S(1)}, f32[1,8,64,256]{3,2,1,0:T(8,128)S(1)}, f32[1,8,64,256]{3,2,1,0:T(8,128)S(1)}) custom-call(s32[16]{0:T(128)S(1)} %copy-done.1, f32[1,16,128,512]{3,2,1,0:T(8,128)} %head.1, f32[1,16,128,512]{3,2,1,0:T(8,128)} %cond.1, f32[1,8,64,256]{3,2,1,0:T(8,128)S(1)} %copy-done), custom_call_target="tpu_custom_call" | custom-call | tf_op jit(solution)/shard_map/pallas_call | solution.py:487
  69.1 2.0 %copy.10 = f32[1,16,128,512]{3,2,1,0:T(8,128)} copy(f32[1,16,128,512]{3,2,1,0:T(8,128)S(1)} %get-tuple-element.6) | data formatting | bytes 8388608
  71.1 0.8 %copy.11 = f32[1,8,64,256]{3,2,1,0:T(8,128)} copy(f32[1,8,64,256]{3,2,1,0:T(8,128)S(1)} %get-tuple-element.7) | data formatting | bytes 1048576
  71.9 0.8 %copy.12 = f32[1,8,64,256]{3,2,1,0:T(8,128)} copy(f32[1,8,64,256]{3,2,1,0:T(8,128)S(1)} %get-tuple-element.8) | data formatting | bytes 1048576
Async XLA Ops:
  0.6 1.0 %copy-start = (f32[1,8,64,256]{3,2,1,0:T(8,128)S(1)}, f32[1,8,64,256]{3,2,1,0:T(8,128)}, u32[]{:S(2)}) copy-start(f32[1,8,64,256]{3,2,1,0:T(8,128)} %ccond.1) | copy-start | bytes 1572868
  1.7 0.7 copy-start.1

commit v2 on v1

v2 whole, which is shorter than its diff:
```python
import functools

import jax
import jax.numpy as jnp
from jax import lax
from jax.experimental import pallas as pl
from jax.experimental.pallas import tpu as pltpu
from jax.sharding import PartitionSpec as P

MESH = pl.DeviceIdType.MESH
F32 = jnp.float32
NP = 8
CAPS = (4, 5, 6, 8)

TOP = 8
CH = 32
NH = 2


FIRST = (0, 7, 1, 2)
SECOND = (3, 4, 5, 6)


def closure(h, cond, spacing):
    t = 1.5 * jnp.minimum(h, 0.0)
    r = lax.rsqrt(1.0 + t * t)
    p = t * r
    a = 1.0 + p
    k = cond * (r * lax.rsqrt(r) * (a * a))
    s2 = spacing * spacing
    w = 1.0 / (20.0 * s2 - (24.0 * s2) * (p * (r * r)))
    return k, w


def in_layer(hb, kb, x, row, rows, spacing):
    ha = hb[x, pl.ds(row, rows + 16), :]
    ka = kb[x, pl.ds(row, rows + 16), :]
    h, k = ha[8 : 8 + rows], ka[8 : 8 + rows]
    tot = (ka[9 : 9 + rows] + k) * (ha[9 : 9 + rows] - h)
    hd, kd = ha[7 : 7 + rows], ka[7 : 7 + rows]
    tot = tot + (kd + k) * (hd - h)
    n = h.shape[1]
    lane = lax.broadcasted_iota(jnp.int32, h.shape, 1)
    hz = jnp.where(lane == n - 1, 0.0, pltpu.roll(h, n - 1, 1))
    kz = jnp.where(lane == n - 1, 0.0, pltpu.roll(k, n - 1, 1))
    hs = h - spacing
    fz = (kz + k) * (hz - hs)
    fd = jnp.where(lane == 0, k * (h + spacing), pltpu.roll(fz, 1, 1))
    return h, k, tot + (fz - fd)


def kernel(cap, pairing_in, head, cond, ccond, fine_out, coarse_out, diff_out,
           hb, kb, wb, fx, f01, f15, frecv, vs, pick, pairing,
           sbuf, sab, sx, sy, sc, sd, tbuf, tab, tx, ty, tc, td, nbuf, nab, nx, ny, nc, nd, mbuf, mab, mx, my, mc, md, bbuf, bab, bx, by, bc, bd,
           ch, ck, cw, cfx, cf01, cf7, cfrecv, dbuf,
           hsem, ksem, csem, osem, halo_s, halo_r, sa_s, sa_r, ta_s, ta_r, na_s, na_r, ma_s, ma_r, ba_s, ba_r, sc_s, sc_r, tc_s, tc_r, nc_s, nc_r, mc_s, mc_r, bc_s, bc_r,
           cross_s, cross_r, psem):
    g = lax.axis_index("group")
    d = lax.axis_index("dom")
    zh = lax.rem(g // 2, 2)
    me = (g // 4) * 2 + lax.rem(g, 2)

    def index_of(j, plane):
        return (j // 2) * 4 + plane * 2 + lax.rem(j, 2)

    def mate(s):
        j = lax.rem(me + s, NP)
        return j, index_of(j, zh)

    other = index_of(me, 1 - zh)
    last = 7

    def load(src, dst, sem):
        return pltpu.make_async_copy(src, dst, sem)

    def hload(l):
        return load(head.at[0, pl.ds(2 * l, 2)], hb.at[pl.ds(2 * l, 2), pl.ds(TOP, 128), :], hsem.at[l])

    def kload(l):
        return load(cond.at[0, pl.ds(2 * l, 2)], kb.at[pl.ds(2 * l, 2), pl.ds(TOP, 128), :], ksem.at[l])

    cload = load(ccond.at[0], ck.at[pl.ds(0, 8), pl.ds(8, 64), :], csem)
    pload = load(pairing_in, pairing, psem)
    hload(0).start()
    kload(0).start()
    pload.start()
    for l in range(1, 8):
        hload(l).start()
    for l in range(1, 8):
        kload(l).start()
    cload.start()

    bar = pltpu.get_barrier_semaphore()

    def greet(g2, d2):
        pl.semaphore_signal(bar, inc=1, device_id=(g2, d2), device_id_type=MESH)

    for s in range(1, NP):
        greet(mate(s)[1], d)
    greet(other, d)

    @pl.when(d > 0)
    def _():
        greet(g, d - 1)

    @pl.when(d < last)
    def _():
        greet(g, d + 1)

    z8 = jnp.zeros((8, 512), F32)
    zc = jnp.zeros((8, 256), F32)

    def pads(x, _):
        for b in (hb, kb):
            b[x, 0:8, :] = z8
            b[x, 136:144, :] = z8
        return 0

    lax.fori_loop(0, 16, pads, 0)

    def cpads(x, _):
        for b in (ch, ck):
            b[x, 0:8, :] = zc
            b[x, 72:80, :] = zc
        return 0

    lax.fori_loop(0, 8, cpads, 0)
    pi = lax.broadcasted_iota(jnp.int32, (256, 128), 0)
    pj = lax.broadcasted_iota(jnp.int32, (256, 128), 1)
    pick[...] = jnp.where(pi // 2 == pj, 0.125, 0.0).astype(jnp.bfloat16)

    @pl.when(d == last)
    def _():
        def zero(i, _):
            hb[16, pl.ds(TOP + i * 8, 8), :] = z8
            kb[16, pl.ds(TOP + i * 8, 8), :] = z8
            return 0

        lax.fori_loop(0, 16, zero, 0)

        def czero(i, _):
            ch[8, pl.ds(8 + i * 8, 8), :] = zc
            ck[8, pl.ds(8 + i * 8, 8), :] = zc
            return 0

        lax.fori_loop(0, 8, czero, 0)

    def remote(src, dst, ssem, rsem, g2, d2):
        return pltpu.make_async_remote_copy(src_ref=src, dst_ref=dst, send_sem=ssem, recv_sem=rsem,
                                            device_id=(g2, d2), device_id_type=MESH)

    down = d - 1
    upper = d + 1

    def part(i, first):
        return pl.ds(first + i * (128 // NH), 128 // NH)

    halo_h = [remote(hb.at[0, part(i, TOP), :], hb.at[16, part(i, TOP), :], halo_s.at[i], halo_r.at[i], g, down) for i in range(NH)]
    halo_k = [remote(kb.at[0, part(i, TOP), :], kb.at[16, part(i, TOP), :], halo_s.at[NH + i], halo_r.at[NH + i], g, down)
              for i in range(NH)]
    halo_f = [remote(f15.at[part(i, 0), :], frecv.at[part(i, 0), :], halo_s.at[2 * NH + i], halo_r.at[2 * NH + i], g, upper)
              for i in range(NH)]
    crow = pl.ds(8, 64)
    chalo_h = remote(ch.at[0, crow, :], ch.at[8, crow, :], halo_s.at[3 * NH], halo_r.at[3 * NH], g, down)
    chalo_k = remote(ck.at[0, crow, :], ck.at[8, crow, :], halo_s.at[3 * NH + 1], halo_r.at[3 * NH + 1], g, down)
    chalo_f = remote(cf7, cfrecv, halo_s.at[3 * NH + 2], halo_r.at[3 * NH + 2], g, upper)

    def on(condition, act):
        pl.when(condition)(act)

    def chunks(act, first=0, rows=128):
        def body(i, _):
            act(pl.multiple_of(first + i * CH, CH))
            return 0

        lax.fori_loop(0, rows // CH, body, 0)

    def halo_start():
        def act():
            for i in range(NH):
                halo_h[i].start()
                halo_k[i].start()

        on(d > 0, act)

    def restrict(a, b, store):
        for r in range(0, 128, CH):
            s = a(r) + b(r)
            for q in range(4):
                vs[q, r : r + CH, :] = s[:, q * 128 : (q + 1) * 128]
        for half in range(2):
            parts = [vs[q, pl.ds(0, 64, 2), :] + vs[q, pl.ds(1, 64, 2), :] for q in (2 * half, 2 * half + 1)]
            e = jnp.concatenate(parts, axis=1)
            hi = e.astype(jnp.bfloat16)
            lo = (e - hi.astype(F32)).astype(jnp.bfloat16)
            w = pick[...]
            o = jnp.dot(hi, w, preferred_element_type=F32) + jnp.dot(lo, w, preferred_element_type=F32)
            store(half, o)

    def into(buf, pos):
        def store(half, o):
            buf[:, pos, :, half * 128 : (half + 1) * 128] = o.reshape(8, 8, 128)

        return store

    def a_copies(p):
        return [remote(p.buf.at[mate(s)[0]], p.ab.at[me], p.a_s.at[s - 1], p.a_r.at[s - 1], mate(s)[1], d) for s in range(1, NP)]

    def a_start(p):
        for c in a_copies(p):
            c.start()
        p.ab[me] = p.buf[me]

    def b_copy(p):
        return remote(p.x, p.y, cross_s.at[p.i], cross_r.at[p.i], other, d)

    def b_start(p):
        for c in a_copies(p):
            c.wait()
        for n in range(cap):
            p.x[n] = p.ab[cross[n]]
        b_copy(p).start()

    def c_copies(p):
        return [remote(p.c.at[mate(s)[0]], p.to.at[me], p.c_s.at[s - 1], p.c_r.at[s - 1], mate(s)[1], d) for s in range(1, NP)]

    def c_start(p):
        b_copy(p).wait()
        for j in range(NP):
            mine, slot, crossed = where[j]
            p.c[j] = jnp.where(mine, p.ab[slot], p.y[crossed])
        for c in c_copies(p):
            c.start()
        p.to[me] = p.c[me]

    def c_wait(p):
        for c in c_copies(p):
            c.wait()

    start = Payload(0, sbuf, sab, sx, sy, sc, sd, sa_s, sa_r, sc_s, sc_r)
    second = Payload(3, tbuf, tab, tx, ty, tc, td, ta_s, ta_r, tc_s, tc_r)
    inner = Payload(1, nbuf, nab, nx, ny, nc, nd, na_s, na_r, nc_s, nc_r)
    more = Payload(4, mbuf, mab, mx, my, mc, md, ma_s, ma_r, mc_s, mc_r)
    outer = Payload(2, bbuf, bab, bx, by, bc, bd, ba_s, ba_r, bc_s, bc_r)

    def spot(l):
        return (start, FIRST.index(l)) if l in FIRST else (second, SECOND.index(l))

    def start_small(l):
        if l:
            hload(l).wait()
        p, pos = spot(l)
        restrict(lambda r: hb[2 * l, pl.ds(TOP + r, CH), :], lambda r: hb[2 * l + 1, pl.ds(TOP + r, CH), :], into(p.buf, pos))

    def close(x):
        def act(r):
            k, w = closure(hb[x, pl.ds(TOP + r, CH), :], kb[x, pl.ds(TOP + r, CH), :], 1.0)
            kb[x, pl.ds(TOP + r, CH), :] = k
            wb[x, pl.ds(r, CH), :] = w

        chunks(act)

    def face(x, r):
        here, there = (x, pl.ds(TOP + r, CH), slice(None)), (x + 1, pl.ds(TOP + r, CH), slice(None))
        return (kb[there] + kb[here]) * (hb[there] - hb[here])

    def first_face():
        def act(r):
            f = face(0, r)
            f01[pl.ds(r, CH), :] = f
            fx[pl.ds(r, CH), :] = f

        chunks(act)

    def step(x):
        def act(r):
            h, k, tot = in_layer(hb, kb, x, r, CH, 1.0)
            f = (kb[x + 1, pl.ds(TOP + r, CH), :] + k) * (hb[x + 1, pl.ds(TOP + r, CH), :] - h)
            tot = tot + (f - fx[pl.ds(r, CH), :])
            fx[pl.ds(r, CH), :] = f
            wb[x, pl.ds(r, CH), :] = h + tot * wb[x, pl.ds(r, CH), :]

        chunks(act)

    def step_between(x, above, below):
        def act(r):
            h, k, tot = in_layer(hb, kb, x, r, CH, 1.0)
            tot = tot + (above[pl.ds(r, CH), :] - below[pl.ds(r, CH), :])
            wb[x, pl.ds(r, CH), :] = h + tot * wb[x, pl.ds(r, CH), :]

        chunks(act)

    def upper_face(i):
        def arrived():
            halo_h[i].wait_recv()
            halo_k[i].wait_recv()

        on(d < last, arrived)

        def act(r):
            f15[pl.ds(r, CH), :] = face(15, r)

        chunks(act, i * (128 // NH), 128 // NH)
        on(d < last, halo_f[i].start)

    def lower_face():
        def arrived():
            for c in halo_f:
                c.wait_recv()

        on(d > 0, arrived)

        def edge():
            def act(r):
                frecv[pl.ds(r, CH), :] = hb[0, pl.ds(TOP + r, CH), :] * kb[0, pl.ds(TOP + r, CH), :]

            chunks(act)

        on(d == 0, edge)

    def out_pair(l):
        return load(wb.at[pl.ds(2 * l, 2)], fine_out.at[0, pl.ds(2 * l, 2)], osem.at[l])

    def next_small(l, buf, pos):
        restrict(lambda r: wb[2 * l, pl.ds(r, CH), :], lambda r: wb[2 * l + 1, pl.ds(r, CH), :], into(buf, pos))
        out_pair(l).start()

    def close_coarse(l):
        p, pos = spot(l)
        h = p.to[:, pos].reshape(64, 256)
        k, w = closure(h, ck[l, crow, :], 2.0)
        ch[l, crow, :] = h
        ck[l, crow, :] = k
        cw[l] = w

    def chalo_start():
        def act():
            chalo_h.start()
            chalo_k.start()

        on(d > 0, act)

    def cface(x):
        return (ck[x + 1, crow, :] + ck[x, crow, :]) * (ch[x + 1, crow, :] - ch[x, crow, :])

    def first_cface():
        f = cface(0)
        cf01[...] = f
        cfx[...] = f

    def step_coarse(x):
        h, k, tot = in_layer(ch, ck, x, 0, 64, 2.0)
        f = cface(x)
        tot = tot + (f - cfx[...])
        cfx[...] = f
        cw[x] = h + tot * cw[x]

    def step_coarse_between(x, above, below):
        h, k, tot = in_layer(ch, ck, x, 0, 64, 2.0)
        cw[x] = h + (tot + (above[...] - below[...])) * cw[x]

    def upper_cface():
        def arrived():
            chalo_h.wait_recv()
            chalo_k.wait_recv()

        on(d < last, arrived)
        cf7[...] = cface(7)
        on(d < last, chalo_f.start)

    def lower_cface():
        on(d > 0, chalo_f.wait_recv)

        def edge():
            cfrecv[...] = ch[0, crow, :] * ck[0, crow, :]

        on(d == 0, edge)

    cout = load(cw, coarse_out.at[0], csem)

    def difference(l, to, pos):
        dbuf[l] = to[:, pos].reshape(64, 256) - cw[l]

    def pair(l):
        if l < 6:
            kload(l + 1).wait()
        close(2 * l + 1)
        close(2 * l + 2)
        step(2 * l)
        step(2 * l + 1)
        next_small(l, nbuf if l < 4 else mbuf, (l - 1) % 3)

    def down_sent():
        for c in halo_h + halo_k:
            c.wait_send()
        chalo_h.wait_send()
        chalo_k.wait_send()

    def up_sent():
        for c in halo_f:
            c.wait_send()
        chalo_f.wait_send()

    hload(0).wait()
    kload(0).wait()
    close(0)
    pload.wait()
    cross = [jnp.int32(0)] * cap
    count = jnp.int32(0)
    for j in range(NP):
        p = pairing[index_of(j, 1 - zh)]
        mine = lax.rem(p // 2, 2) == zh
        slot = (p // 4) * 2 + lax.rem(p, 2)
        for i in range(cap):
            cross[i] = jnp.where(mine & (count == i), slot, cross[i])
        count = count + jnp.where(mine, 1, 0)
    where = []
    count = jnp.int32(0)
    for j in range(NP):
        p = pairing[index_of(j, zh)]
        mine = lax.rem(p // 2, 2) == zh
        where.append((mine, (p // 4) * 2 + lax.rem(p, 2), jnp.minimum(count, cap - 1)))
        count = count + jnp.where(mine, 0, 1)

    for l in FIRST[:1]:
        start_small(l)
    pl.semaphore_wait(bar, NP + jnp.where(d > 0, 1, 0) + jnp.where(d < last, 1, 0))
    halo_start()
    for l in FIRST[1:]:
        start_small(l)
    a_start(start)
    for l in SECOND:
        start_small(l)
    a_start(second)
    close(1)
    first_face()
    kload(7).wait()
    close(15)
    kload(1).wait()
    close(2)
    step(1)
    pair(1)
    pair(2)
    pair(3)
    a_start(inner)
    b_start(start)
    upper_face(0)
    pair(4)
    b_start(second)
    pair(5)
    pair(6)
    a_start(more)
    b_start(inner)
    c_start(start)
    upper_face(1)
    step(14)
    c_start(second)
    step_between(15, f15, fx)
    next_small(7, bbuf, 1)
    c_wait(start)
    cload.wait()
    for l in FIRST:
        close_coarse(l)
    chalo_start()
    b_start(more)
    c_start(inner)
    lower_face()
    step_between(0, f01, frecv)
    next_small(0, bbuf, 0)
    a_start(outer)
    c_wait(second)
    for l in SECOND:
        close_coarse(l)
    first_cface()
    for x in range(1, 7):
        step_coarse(x)
    b_start(outer)
    upper_cface()
    step_coarse_between(7, cf7, cfx)
    c_wait(inner)
    for l in range(1, 4):
        difference(l, nd, l - 1)
    c_start(more)
    c_start(outer)
    lower_cface()
    step_coarse_between(0, cf01, cfrecv)
    cout.start()
    c_wait(more)
    for l in range(4, 7):
        difference(l, md, l - 4)
    dout = [
        load(dbuf.at[pl.ds(1, 6)], diff_out.at[0, pl.ds(1, 6)], ksem.at[0]),
        load(dbuf.at[0], diff_out.at[0, 0], ksem.at[1]),
        load(dbuf.at[7], diff_out.at[0, 7], ksem.at[2]),
    ]
    dout[0].start()
    for l in range(8):
        out_pair(l).wait()
    cout.wait()
    on(d > 0, down_sent)
    on(d < last, up_sent)
    c_wait(outer)
    difference(0, bd, 0)
    dout[1].start()
    difference(7, bd, 1)
    dout[2].start()
    for c in dout:
        c.wait()


class Payload:
    def __init__(self, i, buf, ab, x, y, c, to, a_s, a_r, c_s, c_r):
        self.i, self.buf, self.ab, self.x, self.y, self.c, self.to = i, buf, ab, x, y, c, to
        self.a_s, self.a_r, self.c_s, self.c_r = a_s, a_r, c_s, c_r


def payload(cap, layers):
    piece = (layers, 8, 256)
    return [
        pltpu.VMEM((NP,) + piece, F32),
        pltpu.VMEM((NP,) + piece, F32),
        pltpu.VMEM((cap,) + piece, F32),
        pltpu.VMEM((cap,) + piece, F32),
        pltpu.VMEM((NP,) + piece, F32),
        pltpu.VMEM((NP,) + piece, F32),
    ]


def run(cap, pairing, head, cond, ccond):
    dma = pltpu.SemaphoreType.DMA
    scratch = [
        pltpu.VMEM((17, 144, 512), F32),
        pltpu.VMEM((17, 144, 512), F32),
        pltpu.VMEM((16, 128, 512), F32),
        *[pltpu.VMEM((128, 512), F32)] * 4,
        pltpu.VMEM((4, 128, 128), F32),
        pltpu.VMEM((256, 128), jnp.bfloat16),
        pltpu.SMEM((16,), jnp.int32),
        *payload(cap, 4),
        *payload(cap, 4),
        *payload(cap, 3),
        *payload(cap, 3),
        *payload(cap, 2),
        pltpu.VMEM((9, 80, 256), F32),
        pltpu.VMEM((9, 80, 256), F32),
        pltpu.VMEM((8, 64, 256), F32),
        *[pltpu.VMEM((64, 256), F32)] * 4,
        pltpu.VMEM((8, 64, 256), F32),
        dma((8,)), dma((8,)), dma, dma((8,)), dma((3 * NH + 3,)), dma((3 * NH + 3,)),
        *[dma((NP - 1,))] * 20,
        dma((5,)), dma((5,)), dma,
    ]
    anywhere = pl.BlockSpec(memory_space=pl.ANY)
    return pl.pallas_call(
        functools.partial(kernel, cap),
        out_shape=(
            jax.ShapeDtypeStruct(head.shape, F32),
            jax.ShapeDtypeStruct(ccond.shape, F32),
            jax.ShapeDtypeStruct(ccond.shape, F32),
        ),
        in_specs=[pl.BlockSpec(memory_space=pltpu.HBM)] * 4,
        out_specs=(anywhere, anywhere, anywhere),
        scratch_shapes=scratch,
        compiler_params=pltpu.CompilerParams(
            collective_id=cap, has_side_effects=True, vmem_limit_bytes=48 * 2**20
        ),
    )(*[pltpu.with_memory_space_constraint(v, pltpu.HBM) for v in (pairing, head, cond, ccond)])


def write_out(fine, coarse, diff, fine_out, coarse_out, diff_out, sem):
    copies = [pltpu.make_async_copy(fine.at[0, pl.ds(4 * i, 4)], fine_out.at[0, pl.ds(4 * i, 4)], sem.at[i]) for i in range(4)]
    copies.append(pltpu.make_async_copy(coarse, coarse_out, sem.at[4]))
    copies.append(pltpu.make_async_copy(diff, diff_out, sem.at[5]))
    for c in copies:
        c.start()
    for c in copies:
        c.wait()


def finish(*results):
    anywhere = pl.BlockSpec(memory_space=pl.ANY)
    return pl.pallas_call(
        write_out,
        out_shape=tuple(pltpu.HBM(r.shape, r.dtype) for r in results),
        in_specs=[anywhere] * 3,
        out_specs=(anywhere,) * 3,
        scratch_shapes=[pltpu.SemaphoreType.DMA((6,))],
        compiler_params=pltpu.CompilerParams(vmem_limit_bytes=2**20),
    )(*[pltpu.with_memory_space_constraint(r, pltpu.VMEM) for r in results])


def whole(cap, *arrays):
    return finish(*run(cap, *arrays))


def per_device(head, conductivity, coarse_conductivity, pairing):
    i = jnp.arange(16)
    crossing = jnp.where((i // 2) % 2 == 0, (pairing // 2) % 2, 0) - jnp.where(i == 0, CAPS[0], 0)
    kernels = [functools.partial(whole, cap) for cap in CAPS]
    return lax.switch(jnp.sum(crossing), kernels, pairing, head, conductivity, coarse_conductivity)


def solution(mesh):
    block = P("group", "dom", None, None)
    return jax.shard_map(
        per_device,
        mesh=mesh,
        in_specs=(block, block, block, P()),
        out_specs=(block, block, block),
        check_vma=False,
    )
```

time: 72.8 us -> 56.2 us (0.77)
  the two profiles are of different devices: /device:TPU:1 before, /device:TPU:35 now
where the time goes in v2:
time: 56.2 us; the launch traced here: 56.1 us
  Pallas kernels  52.7 us (94%)
  between operations  1.5 us (3%)
  other arithmetic  1.31 us (2%)
    pallas_call x1, Pallas kernels, run(): pl.pallas_call(functools.partial(kernel, cap), out_shape=(jax.ShapeDtypeS...  50.4 us
    pallas_call x1, Pallas kernels, finish(): pl.pallas_call(write_out, out_shape=tuple((pltpu.HBM(r.shape, r.dtype) fo...  2.39 us
    reduce_sum x1, other arithmetic, per_device(): jnp.sum(crossing)  1.31 us

profile of v2, /device:TPU:35, one launch (start us, length us, event | category | flops | bytes accessed | tf_op | source)
XLA Modules:
  0.0 56.1 jit_solution(5244645252301065908)
XLA Ops:
  0.6 1.3 %fusion.3 = s32[]{:T(128)} fusion(s32[16]{0:T(128)} %param.11), kind=kLoop, calls=%fused_computation.19 | loop fusion | flops 815 | bytes 68 | tf_op jit(solution)/shard_map/reduce_sum | solution.py:600
  2.6 53.3 %conditional.1 = ((f32[1,16,128,512]{3,2,1,0:T(8,128)}, f32[1,8,64,256]{3,2,1,0:T(8,128)}, f32[1,8,64,256]{3,2,1,0:T(8,128)})) conditional(s32[]{:T(128)} %clamp.3, (s32[16]{0:T(128)}, f32[1,16,128,512]{3,2,1,0:T(8,128)}, f32[1,16,128,512]{3,2,1,0:T(8,128)}, f32[1,8,64,256]{3,2,1,0:T(8,128)}) %tuple.19, ...), branch_computations={%region_1.2_spmd, %region_2.3_spmd, %region_3.4_spmd, %region_4.5_... | conditional | bytes 8 | solution.py:600
  2.6 50.4 %branch_0_fun.2 = (f32[1,16,128,512]{3,2,1,0:T(8,128)S(1)}, f32[1,8,64,256]{3,2,1,0:T(8,128)S(1)}, f32[1,8,64,256]{3,2,1,0:T(8,128)S(1)}) custom-call(s32[16]{0:T(128)} %get-tuple-element.32.pairing_in, f32[1,16,128,512]{3,2,1,0:T(8,128)} %get-tuple-element.33.head, f32[1,16,128,512]{3,2,1,0:T(8,128)} %get-tuple-element.34.cond, ...), custom_call_target="tpu_custom_call" | custom-call | tf_op jit(solution)/shard_map/cond/branch_0_fun/pallas_call | solution.py:554
  53.0 2.4 %branch_0_fun.3 = (f32[1,16,128,512]{3,2,1,0:T(8,128)}, f32[1,8,64,256]{3,2,1,0:T(8,128)}, f32[1,8,64,256]{3,2,1,0:T(8,128)}) custom-call(f32[1,16,128,512]{3,2,1,0:T(8,128)S(1)} %get-tuple-element.36.fine, f32[1,8,64,256]{3,2,1,0:T(8,128)S(1)} %get-tuple-element.37.coarse, f32[1,8,64,256]{3,2,1,0:T(8,128)S(1)} %get-tuple-element.38.diff), custom_call_target="tpu_custom_call" | custom-call | tf_op jit(solution)/shard_map/cond/branch_0_fun/pallas_call | solution.py:582

commit v3 on v2

--- a/solution.py
+++ b/solution.py
@@ -10,7 +10,7 @@
 MESH = pl.DeviceIdType.MESH
 F32 = jnp.float32
 NP = 8
-CAPS = (4, 5, 6, 8)
+CAPS = (3, 4, 5, 6, 8)
 
 TOP = 8
 CH = 32
@@ -50,11 +50,12 @@
 
 
 def kernel(cap, pairing_in, head, cond, ccond, fine_out, coarse_out, diff_out,
-           hb, kb, wb, fx, f01, f15, frecv, vs, pick, pairing,
+           hb, kb, fx, f01, f15, frecv, vs, pick, pairing,
            sbuf, sab, sx, sy, sc, sd, tbuf, tab, tx, ty, tc, td, nbuf, nab, nx, ny, nc, nd, mbuf, mab, mx, my, mc, md, bbuf, bab, bx, by, bc, bd,
-           ch, ck, cw, cfx, cf01, cf7, cfrecv, dbuf,
-           hsem, ksem, csem, osem, halo_s, halo_r, sa_s, sa_r, ta_s, ta_r, na_s, na_r, ma_s, ma_r, ba_s, ba_r, sc_s, sc_r, tc_s, tc_r, nc_s, nc_r, mc_s, mc_r, bc_s, bc_r,
+           ch, ck, cfx, cf01, cf7, cfrecv,
+           hsem, ksem, csem, halo_s, halo_r, sa_s, sa_r, ta_s, ta_r, na_s, na_r, ma_s, ma_r, ba_s, ba_r, sc_s, sc_r, tc_s, tc_r, nc_s, nc_r, mc_s, mc_r, bc_s, bc_r,
            cross_s, cross_r, psem):
+    wb, cw, dbuf = fine_out.at[0], coarse_out.at[0], diff_out.at[0]
     g = lax.axis_index("group")
     d = lax.axis_index("dom")
     zh = lax.rem(g // 2, 2)
@@ -80,6 +81,23 @@
         return load(cond.at[0, pl.ds(2 * l, 2)], kb.at[pl.ds(2 * l, 2), pl.ds(TOP, 128), :], ksem.at[l])
 
     cload = load(ccond.at[0], ck.at[pl.ds(0, 8), pl.ds(8, 64), :], csem)
+    bar = pltpu.get_barrier_semaphore()
+
+    def greet(g2, d2):
+        pl.semaphore_signal(bar, inc=1, device_id=(g2, d2), device_id_type=MESH)
+
+    for s in range(1, NP):
+        greet(mate(s)[1], d)
+    greet(other, d)
+
+    @pl.when(d > 0)
+    def _():
+        greet(g, d - 1)
+
+    @pl.when(d < last)
+    def _():
+        greet(g, d + 1)
+
     pload = load(pairing_in, pairing, psem)
     hload(0).start()
     kload(0).start()
@@ -89,61 +107,6 @@
     for l in range(1, 8):
         kload(l).start()
     cload.start()
-
-    bar = pltpu.get_barrier_semaphore()
-
-    def greet(g2, d2):
-        pl.semaphore_signal(bar, inc=1, device_id=(g2, d2), device_id_type=MESH)
-
-    for s in range(1, NP):
-        greet(mate(s)[1], d)
-    greet(other, d)
-
-    @pl.when(d > 0)
-    def _():
-        greet(g, d - 1)
-
-    @pl.when(d < last)
-    def _():
-        greet(g, d + 1)
-
-    z8 = jnp.zeros((8, 512), F32)
-    zc = jnp.zeros((8, 256), F32)
-
-    def pads(x, _):
-        for b in (hb, kb):
-            b[x, 0:8, :] = z8
-            b[x, 136:144, :] = z8
-        return 0
-
-    lax.fori_loop(0, 16, pads, 0)
-
-    def cpads(x, _):
-        for b in (ch, ck):
-            b[x, 0:8, :] = zc
-            b[x, 72:80, :] = zc
-        return 0
-
-    lax.fori_loop(0, 8, cpads, 0)
-    pi = lax.broadcasted_iota(jnp.int32, (256, 128), 0)
-    pj = lax.broadcasted_iota(jnp.int32, (256, 128), 1)
-    pick[...] = jnp.where(pi // 2 == pj, 0.125, 0.0).astype(jnp.bfloat16)
-
-    @pl.when(d == last)
-    def _():
-        def zero(i, _):
-            hb[16, pl.ds(TOP + i * 8, 8), :] = z8
-            kb[16, pl.ds(TOP + i * 8, 8), :] = z8
-            return 0
-
-        lax.fori_loop(0, 16, zero, 0)
-
-        def czero(i, _):
-            ch[8, pl.ds(8 + i * 8, 8), :] = zc
-            ck[8, pl.ds(8 + i * 8, 8), :] = zc
-            return 0
-
-        lax.fori_loop(0, 8, czero, 0)
 
     def remote(src, dst, ssem, rsem, g2, d2):
         return pltpu.make_async_remote_copy(src_ref=src, dst_ref=dst, send_sem=ssem, recv_sem=rsem,
@@ -203,39 +166,37 @@
 
         return store
 
-    def a_copies(p):
-        return [remote(p.buf.at[mate(s)[0]], p.ab.at[me], p.a_s.at[s - 1], p.a_r.at[s - 1], mate(s)[1], d) for s in range(1, NP)]
+    def scatter(buf, to, ssem, rsem):
+        for s in range(1, NP):
+            j, g2 = mate(s)
+            remote(buf.at[j], to.at[me], ssem, rsem, g2, d).start()
+        to[me] = buf[me]
+
+    def scattered(buf, to, ssem, rsem):
+        most = pl.ds(0, NP - 1)
+        remote(buf.at[most], to.at[most], ssem, rsem, mate(1)[1], d).wait()
 
     def a_start(p):
-        for c in a_copies(p):
-            c.start()
-        p.ab[me] = p.buf[me]
+        scatter(p.buf, p.ab, p.a_s, p.a_r)
 
     def b_copy(p):
         return remote(p.x, p.y, cross_s.at[p.i], cross_r.at[p.i], other, d)
 
     def b_start(p):
-        for c in a_copies(p):
-            c.wait()
+        scattered(p.buf, p.ab, p.a_s, p.a_r)
         for n in range(cap):
             p.x[n] = p.ab[cross[n]]
         b_copy(p).start()
-
-    def c_copies(p):
-        return [remote(p.c.at[mate(s)[0]], p.to.at[me], p.c_s.at[s - 1], p.c_r.at[s - 1], mate(s)[1], d) for s in range(1, NP)]
 
     def c_start(p):
         b_copy(p).wait()
         for j in range(NP):
             mine, slot, crossed = where[j]
             p.c[j] = jnp.where(mine, p.ab[slot], p.y[crossed])
-        for c in c_copies(p):
-            c.start()
-        p.to[me] = p.c[me]
+        scatter(p.c, p.to, p.c_s, p.c_r)
 
     def c_wait(p):
-        for c in c_copies(p):
-            c.wait()
+        scattered(p.c, p.to, p.c_s, p.c_r)
 
     start = Payload(0, sbuf, sab, sx, sy, sc, sd, sa_s, sa_r, sc_s, sc_r)
     second = Payload(3, tbuf, tab, tx, ty, tc, td, ta_s, ta_r, tc_s, tc_r)
@@ -318,12 +279,8 @@
 
         on(d == 0, edge)
 
-    def out_pair(l):
-        return load(wb.at[pl.ds(2 * l, 2)], fine_out.at[0, pl.ds(2 * l, 2)], osem.at[l])
-
     def next_small(l, buf, pos):
         restrict(lambda r: wb[2 * l, pl.ds(r, CH), :], lambda r: wb[2 * l + 1, pl.ds(r, CH), :], into(buf, pos))
-        out_pair(l).start()
 
     def close_coarse(l):
         p, pos = spot(l)
@@ -375,8 +332,6 @@
             cfrecv[...] = ch[0, crow, :] * ck[0, crow, :]
 
         on(d == 0, edge)
-
-    cout = load(cw, coarse_out.at[0], csem)
 
     def difference(l, to, pos):
         dbuf[l] = to[:, pos].reshape(64, 256) - cw[l]
@@ -422,10 +377,48 @@
         where.append((mine, (p // 4) * 2 + lax.rem(p, 2), jnp.minimum(count, cap - 1)))
         count = count + jnp.where(mine, 0, 1)
 
+    pi = lax.broadcasted_iota(jnp.int32, (256, 128), 0)
+    pj = lax.broadcasted_iota(jnp.int32, (256, 128), 1)
+    pick[...] = jnp.where(pi // 2 == pj, 0.125, 0.0).astype(jnp.bfloat16)
+
     for l in FIRST[:1]:
         start_small(l)
     pl.semaphore_wait(bar, NP + jnp.where(d > 0, 1, 0) + jnp.where(d < last, 1, 0))
     halo_start()
+    z8 = jnp.zeros((8, 512), F32)
+    zc = jnp.zeros((8, 256), F32)
+
+    def pads(x, _):
+        for b in (hb, kb):
+            b[x, 0:8, :] = z8
+            b[x, 136:144, :] = z8
+        return 0
+
+    lax.fori_loop(0, 16, pads, 0)
+
+    def cpads(x, _):
+        for b in (ch, ck):
+            b[x, 0:8, :] = zc
+            b[x, 72:80, :] = zc
+        return 0
+
+    lax.fori_loop(0, 8, cpads, 0)
+    @pl.when(d == last)
+    def _():
+        def zero(i, _):
+            hb[16, pl.ds(TOP + i * 8, 8), :] = z8
+            kb[16, pl.ds(TOP + i * 8, 8), :] = z8
+            return 0
+
+        lax.fori_loop(0, 16, zero, 0)
+
+        def czero(i, _):
+            ch[8, pl.ds(8 + i * 8, 8), :] = zc
+            ck[8, pl.ds(8 + i * 8, 8), :] = zc
+            return 0
+
+        lax.fori_loop(0, 8, czero, 0)
+
     for l in FIRST[1:]:
         start_small(l)
     a_start(start)
@@ -484,28 +477,14 @@
     c_start(outer)
     lower_cface()
     step_coarse_between(0, cf01, cfrecv)
-    cout.start()
     c_wait(more)
     for l in range(4, 7):
         difference(l, md, l - 4)
-    dout = [
-        load(dbuf.at[pl.ds(1, 6)], diff_out.at[0, pl.ds(1, 6)], ksem.at[0]),
-        load(dbuf.at[0], diff_out.at[0, 0], ksem.at[1]),
-        load(dbuf.at[7], diff_out.at[0, 7], ksem.at[2]),
-    ]
-    dout[0].start()
-    for l in range(8):
-        out_pair(l).wait()
-    cout.wait()
     on(d > 0, down_sent)
     on(d < last, up_sent)
     c_wait(outer)
     difference(0, bd, 0)
-    dout[1].start()
     difference(7, bd, 1)
-    dout[2].start()
-    for c in dout:
-        c.wait()
 
 
 class Payload:
@@ -531,7 +510,6 @@
     scratch = [
         pltpu.VMEM((17, 144, 512), F32),
         pltpu.VMEM((17, 144, 512), F32),
-        pltpu.VMEM((16, 128, 512), F32),
         *[pltpu.VMEM((128, 512), F32)] * 4,
         pltpu.VMEM((4, 128, 128), F32),
         pltpu.VMEM((256, 128), jnp.bfloat16),
@@ -543,23 +521,16 @@
         *payload(cap, 2),
         pltpu.VMEM((9, 80, 256), F32),
         pltpu.VMEM((9, 80, 256), F32),
-        pltpu.VMEM((8, 64, 256), F32),
         *[pltpu.VMEM((64, 256), F32)] * 4,
-        pltpu.VMEM((8, 64, 256), F32),
-        dma((8,)), dma((8,)), dma, dma((8,)), dma((3 * NH + 3,)), dma((3 * NH + 3,)),
-        *[dma((NP - 1,))] * 20,
+        dma((8,)), dma((8,)), dma, dma((3 * NH + 3,)), dma((3 * NH + 3,)),
+        *[dma] * 20,
         dma((5,)), dma((5,)), dma,
     ]
-    anywhere = pl.BlockSpec(memory_space=pl.ANY)
     return pl.pallas_call(
         functools.partial(kernel, cap),
-        out_shape=(
-            jax.ShapeDtypeStruct(head.shape, F32),
-            jax.ShapeDtypeStruct(ccond.shape, F32),
-            jax.ShapeDtypeStruct(ccond.shape, F32),
-        ),
+        out_shape=(pltpu.VMEM(head.shape, F32), pltpu.VMEM(ccond.shape, F32), pltpu.VMEM(ccond.shape, F32)),
         in_specs=[pl.BlockSpec(memory_space=pltpu.HBM)] * 4,
-        out_specs=(anywhere, anywhere, anywhere),
+        out_specs=(pl.BlockSpec(memory_space=pltpu.VMEM),) * 3,
         scratch_shapes=scratch,
         compiler_params=pltpu.CompilerParams(
             collective_id=cap, has_side_effects=True, vmem_limit_bytes=48 * 2**20

time: 56.2 us -> 52.9 us (0.941)
  the two profiles are of different devices: /device:TPU:35 before, /device:TPU:1 now
where the time goes in v3:
time: 52.9 us; the launch traced here: 52.6 us
  Pallas kernels  49.2 us (93%)
  between operations  1.5 us (3%)
  other arithmetic  1.31 us (2%)
  loops' own time  0.56 us (1%)
    pallas_call x1, Pallas kernels, run(): pl.pallas_call(functools.partial(kernel, cap), out_shape=(pltpu.VMEM(head...  46.8 us
    pallas_call x1, Pallas kernels, finish(): pl.pallas_call(write_out, out_shape=tuple((pltpu.HBM(r.shape, r.dtype) fo...  2.39 us
    reduce_sum x1, other arithmetic, per_device(): jnp.sum(crossing)  1.31 us

profile of v3, /device:TPU:1, one launch (start us, length us, event | category | flops | bytes accessed | tf_op | source)
XLA Modules:
  0.0 52.6 jit_solution(18270267025405205619)
XLA Ops:
  0.6 1.3 %fusion.3 = s32[]{:T(128)} fusion(s32[16]{0:T(128)} %param.12), kind=kLoop, calls=%fused_computation.19 | loop fusion | flops 815 | bytes 68 | tf_op jit(solution)/shard_map/reduce_sum | solution.py:571
  2.6 49.8 %conditional.1 = ((f32[1,16,128,512]{3,2,1,0:T(8,128)}, f32[1,8,64,256]{3,2,1,0:T(8,128)}, f32[1,8,64,256]{3,2,1,0:T(8,128)})) conditional(s32[]{:T(128)} %clamp.3, (s32[16]{0:T(128)}, f32[1,16,128,512]{3,2,1,0:T(8,128)}, f32[1,16,128,512]{3,2,1,0:T(8,128)}, f32[1,8,64,256]{3,2,1,0:T(8,128)}) %tuple.22, ...), branch_computations={%region_1.2_spmd, %region_2.3_spmd, %region_3.4_spmd, %region_4.5_... | conditional | bytes 8 | solution.py:571
  2.6 46.8 %branch_0_fun.2 = (f32[1,16,128,512]{3,2,1,0:T(8,128)S(1)}, f32[1,8,64,256]{3,2,1,0:T(8,128)S(1)}, f32[1,8,64,256]{3,2,1,0:T(8,128)S(1)}) custom-call(s32[16]{0:T(128)} %get-tuple-element.40.pairing_in, f32[1,16,128,512]{3,2,1,0:T(8,128)} %get-tuple-element.41.head, f32[1,16,128,512]{3,2,1,0:T(8,128)} %get-tuple-element.42.cond, ...), custom_call_target="tpu_custom_call" | custom-call | tf_op jit(solution)/shard_map/cond/branch_0_fun/pallas_call | solution.py:529
  49.4 2.4 %branch_0_fun.3 = (f32[1,16,128,512]{3,2,1,0:T(8,128)}, f32[1,8,64,256]{3,2,1,0:T(8,128)}, f32[1,8,64,256]{3,2,1,0:T(8,128)}) custom-call(f32[1,16,128,512]{3,2,1,0:T(8,128)S(1)} %get-tuple-element.44.fine, f32[1,8,64,256]{3,2,1,0:T(8,128)S(1)} %get-tuple-element.45.coarse, f32[1,8,64,256]{3,2,1,0:T(8,128)S(1)} %get-tuple-element.46.diff), custom_call_target="tpu_custom_call" | custom-call | tf_op jit(solution)/shard_map/cond/branch_0_fun/pallas_call | solution.py:553

commit v4 on v3

--- a/solution.py
+++ b/solution.py
@@ -343,7 +343,7 @@
         close(2 * l + 2)
         step(2 * l)
         step(2 * l + 1)
-        next_small(l, nbuf if l < 4 else mbuf, (l - 1) % 3)
+        next_small(l, nbuf if l < 5 else mbuf, (l - 1) % 4)
 
     def down_sent():
         for c in halo_h + halo_k:
@@ -435,51 +435,51 @@
     pair(1)
     pair(2)
     pair(3)
-    a_start(inner)
     b_start(start)
     upper_face(0)
     pair(4)
+    a_start(inner)
     b_start(second)
     pair(5)
+    upper_face(1)
     pair(6)
     a_start(more)
     b_start(inner)
-    c_start(start)
-    upper_face(1)
     step(14)
-    c_start(second)
     step_between(15, f15, fx)
     next_small(7, bbuf, 1)
+    c_start(start)
+    lower_face()
+    step_between(0, f01, frecv)
+    next_small(0, bbuf, 0)
+    a_start(outer)
+    b_start(more)
     c_wait(start)
     cload.wait()
     for l in FIRST:
         close_coarse(l)
+    b_start(outer)
     chalo_start()
-    b_start(more)
+    c_start(second)
     c_start(inner)
-    lower_face()
-    step_between(0, f01, frecv)
-    next_small(0, bbuf, 0)
-    a_start(outer)
+    c_start(more)
+    c_start(outer)
     c_wait(second)
     for l in SECOND:
         close_coarse(l)
     first_cface()
     for x in range(1, 7):
         step_coarse(x)
-    b_start(outer)
     upper_cface()
     step_coarse_between(7, cf7, cfx)
     c_wait(inner)
-    for l in range(1, 4):
+    for l in range(1, 5):
         difference(l, nd, l - 1)
-    c_start(more)
-    c_start(outer)
+    c_wait(more)
+    for l in range(5, 7):
+        difference(l, md, l - 5)
     lower_cface()
     step_coarse_between(0, cf01, cfrecv)
-    c_wait(more)
-    for l in range(4, 7):
-        difference(l, md, l - 4)
     on(d > 0, down_sent)
     on(d < last, up_sent)
     c_wait(outer)
@@ -516,8 +516,8 @@
         pltpu.SMEM((16,), jnp.int32),
         *payload(cap, 4),
         *payload(cap, 4),
-        *payload(cap, 3),
-        *payload(cap, 3),
+        *payload(cap, 4),
+        *payload(cap, 2),
         *payload(cap, 2),
         pltpu.VMEM((9, 80, 256), F32),
         pltpu.VMEM((9, 80, 256), F32),

time: 52.9 us -> 52 us (0.983)
  the two profiles are of different devices: /device:TPU:1 before, /device:TPU:3 now
where the time goes in v4:
time: 52 us; the launch traced here: 51.9 us
  Pallas kernels  48.5 us (93%)
  between operations  1.5 us (3%)
  other arithmetic  1.31 us (3%)
  loops' own time  0.56 us (1%)
    pallas_call x1, Pallas kernels, run(): pl.pallas_call(functools.partial(kernel, cap), out_shape=(pltpu.VMEM(head...  46.1 us
    pallas_call x1, Pallas kernels, finish(): pl.pallas_call(write_out, out_shape=tuple((pltpu.HBM(r.shape, r.dtype) fo...  2.39 us
    reduce_sum x1, other arithmetic, per_device(): jnp.sum(crossing)  1.31 us

profile of v4, /device:TPU:3, one launch (start us, length us, event | category | flops | bytes accessed | tf_op | source)
XLA Modules:
  0.0 51.9 jit_solution(403495839056345399)
XLA Ops:
  0.6 1.3 %fusion.3 = s32[]{:T(128)} fusion(s32[16]{0:T(128)} %param.12), kind=kLoop, calls=%fused_computation.19 | loop fusion | flops 815 | bytes 68 | tf_op jit(solution)/shard_map/reduce_sum | solution.py:571
  2.6 49.0 %conditional.1 = ((f32[1,16,128,512]{3,2,1,0:T(8,128)}, f32[1,8,64,256]{3,2,1,0:T(8,128)}, f32[1,8,64,256]{3,2,1,0:T(8,128)})) conditional(s32[]{:T(128)} %clamp.3, (s32[16]{0:T(128)}, f32[1,16,128,512]{3,2,1,0:T(8,128)}, f32[1,16,128,512]{3,2,1,0:T(8,128)}, f32[1,8,64,256]{3,2,1,0:T(8,128)}) %tuple.22, ...), branch_computations={%region_1.2_spmd, %region_2.3_spmd, %region_3.4_spmd, %region_4.5_... | conditional | bytes 8 | solution.py:571
  2.6 46.1 %branch_0_fun.2 = (f32[1,16,128,512]{3,2,1,0:T(8,128)S(1)}, f32[1,8,64,256]{3,2,1,0:T(8,128)S(1)}, f32[1,8,64,256]{3,2,1,0:T(8,128)S(1)}) custom-call(s32[16]{0:T(128)} %get-tuple-element.40.pairing_in, f32[1,16,128,512]{3,2,1,0:T(8,128)} %get-tuple-element.41.head, f32[1,16,128,512]{3,2,1,0:T(8,128)} %get-tuple-element.42.cond, ...), custom_call_target="tpu_custom_call" | custom-call | tf_op jit(solution)/shard_map/cond/branch_0_fun/pallas_call | solution.py:529
  48.7 2.4 %branch_0_fun.3 = (f32[1,16,128,512]{3,2,1,0:T(8,128)}, f32[1,8,64,256]{3,2,1,0:T(8,128)}, f32[1,8,64,256]{3,2,1,0:T(8,128)}) custom-call(f32[1,16,128,512]{3,2,1,0:T(8,128)S(1)} %get-tuple-element.44.fine, f32[1,8,64,256]{3,2,1,0:T(8,128)S(1)} %get-tuple-element.45.coarse, f32[1,8,64,256]{3,2,1,0:T(8,128)S(1)} %get-tuple-element.46.diff), custom_call_target="tpu_custom_call" | custom-call | tf_op jit(solution)/shard_map/cond/branch_0_fun/pallas_call | solution.py:553

commit v5 on v4

--- a/solution.py
+++ b/solution.py
@@ -439,11 +439,11 @@
     upper_face(0)
     pair(4)
     a_start(inner)
-    b_start(second)
     pair(5)
-    upper_face(1)
     pair(6)
     a_start(more)
+    upper_face(1)
+    b_start(second)
     b_start(inner)
     step(14)
     step_between(15, f15, fx)
@@ -458,18 +458,18 @@
     cload.wait()
     for l in FIRST:
         close_coarse(l)
+    c_start(second)
     b_start(outer)
     chalo_start()
-    c_start(second)
     c_start(inner)
-    c_start(more)
-    c_start(outer)
     c_wait(second)
     for l in SECOND:
         close_coarse(l)
     first_cface()
     for x in range(1, 7):
         step_coarse(x)
+    c_start(more)
+    c_start(outer)
     upper_cface()
     step_coarse_between(7, cf7, cfx)
     c_wait(inner)

time: 52 us -> 51.1 us (0.983)
  the two profiles are of different devices: /device:TPU:3 before, /device:TPU:1 now
where the time goes in v5:
time: 51.1 us; the launch traced here: 51 us
  Pallas kernels  47.6 us (93%)
  between operations  1.5 us (3%)
  other arithmetic  1.31 us (3%)
  loops' own time  0.56 us (1%)
    pallas_call x1, Pallas kernels, run(): pl.pallas_call(functools.partial(kernel, cap), out_shape=(pltpu.VMEM(head...  45.3 us
    pallas_call x1, Pallas kernels, finish(): pl.pallas_call(write_out, out_shape=tuple((pltpu.HBM(r.shape, r.dtype) fo...  2.39 us
    reduce_sum x1, other arithmetic, per_device(): jnp.sum(crossing)  1.31 us

profile of v5, /device:TPU:1, one launch (start us, length us, event | category | flops | bytes accessed | tf_op | source)
XLA Modules:
  0.0 51.0 jit_solution(14115127722003332211)
XLA Ops:
  0.6 1.3 %fusion.3 = s32[]{:T(128)} fusion(s32[16]{0:T(128)} %param.12), kind=kLoop, calls=%fused_computation.19 | loop fusion | flops 815 | bytes 68 | tf_op jit(solution)/shard_map/reduce_sum | solution.py:571
  2.6 48.2 %conditional.1 = ((f32[1,16,128,512]{3,2,1,0:T(8,128)}, f32[1,8,64,256]{3,2,1,0:T(8,128)}, f32[1,8,64,256]{3,2,1,0:T(8,128)})) conditional(s32[]{:T(128)} %clamp.3, (s32[16]{0:T(128)}, f32[1,16,128,512]{3,2,1,0:T(8,128)}, f32[1,16,128,512]{3,2,1,0:T(8,128)}, f32[1,8,64,256]{3,2,1,0:T(8,128)}) %tuple.22, ...), branch_computations={%region_1.2_spmd, %region_2.3_spmd, %region_3.4_spmd, %region_4.5_... | conditional | bytes 8 | solution.py:571
  2.6 45.3 %branch_1_fun.2 = (f32[1,16,128,512]{3,2,1,0:T(8,128)S(1)}, f32[1,8,64,256]{3,2,1,0:T(8,128)S(1)}, f32[1,8,64,256]{3,2,1,0:T(8,128)S(1)}) custom-call(s32[16]{0:T(128)} %get-tuple-element.47.pairing_in, f32[1,16,128,512]{3,2,1,0:T(8,128)} %get-tuple-element.48.head, f32[1,16,128,512]{3,2,1,0:T(8,128)} %get-tuple-element.49.cond, ...), custom_call_target="tpu_custom_call" | custom-call | tf_op jit(solution)/shard_map/cond/branch_1_fun/pallas_call | solution.py:529
  47.9 2.4 %branch_1_fun.3 = (f32[1,16,128,512]{3,2,1,0:T(8,128)}, f32[1,8,64,256]{3,2,1,0:T(8,128)}, f32[1,8,64,256]{3,2,1,0:T(8,128)}) custom-call(f32[1,16,128,512]{3,2,1,0:T(8,128)S(1)} %get-tuple-element.51.fine, f32[1,8,64,256]{3,2,1,0:T(8,128)S(1)} %get-tuple-element.52.coarse, f32[1,8,64,256]{3,2,1,0:T(8,128)S(1)} %get-tuple-element.53.diff), custom_call_target="tpu_custom_call" | custom-call | tf_op jit(solution)/shard_map/cond/branch_1_fun/pallas_call | solution.py:553
